TPU v7x, 32 devices: a whole 2x2x4 slice. The times are simulated.
32 devices in a mesh: segment: 2 (over x), dp: 4 (over z), mp: 4 (over y, core).
Axes of the slice: x: 2, y: 2, z: 4, core: 2. Of those that a mesh axis runs over, the one named last changes fastest.
Arguments:
- patch_tokens: bfloat16 [32, 16, 3072], P('dp', None, 'mp'), may hold values from -400 to 400
- visible_index: int32 [32, 16], P('dp'), may hold values from 0 to 63, as said below
- output_grad: bfloat16 [32, 16, 3072], P('dp', None, 'mp'), may hold values from -1.5 to 1.5
- norm_gain: float32 [2, 3072], P('segment'), may hold values from 0.1 to 1.9
- master_weights: float32 [2, 12288, 2048], P('segment', 'dp', 'mp'), may hold values from -2 to 2
- first_moment: float32 [2, 12288, 2048], P('segment', 'dp', 'mp'), may hold values from -6 to 6
- second_moment: float32 [2, 12288, 2048], P('segment', 'dp', 'mp'), may hold values from 0.01 to 1
Outputs:
- new_master: float32 [2, 12288, 2048], P('segment', 'dp', 'mp')
- new_first: float32 [2, 12288, 2048], P('segment', 'dp', 'mp')
- new_second: float32 [2, 12288, 2048], P('segment', 'dp', 'mp')
Inputs may be any that keep to these rules, and one draw needn't show every extreme that they name: `visible_index`: in each volume the 16 indices are distinct and increasing.
All inputs are finite; a program needn't handle non-finite values.
Results may differ from a plain program's by a relative error of at most 0.02.
Values may be sent and summed in bfloat16 or wider, within the bound.
A program may use at most 192 MiB of HBM per device.

v0:
```python
import math
import jax
import jax.numpy as jnp
from jax import lax
from jax.sharding import PartitionSpec as P

HD = 128
MB_VOLS = 2
beta_one = 0.9
beta_two = 0.95
learn_rate = 0.01
decay_rate = 0.1
adam_eps = 1e-08
norm_eps = 1e-05
step_count = 10


def from_behind(array, axis, by):
    peers = lax.axis_size(axis)
    pairs = [(i, i + by) for i in range(peers) if 0 <= i + by < peers]
    return lax.ppermute(array, axis, pairs)


def position_table(visible_index, model_width):
    half_width = model_width // 2
    angle_rate = jnp.exp(
        jnp.arange(half_width, dtype=jnp.float32) * (-2.0 * math.log(10000.0) / model_width)
    )
    angles = visible_index.astype(jnp.float32)[..., None] * angle_rate
    return jnp.concatenate([jnp.sin(angles), jnp.cos(angles)], axis=-1)


def norm_forward(hidden, norm_scale):
    values = hidden.astype(jnp.float32)
    centred = values - jnp.mean(values, axis=-1, keepdims=True)
    inverse_dev = lax.rsqrt(jnp.mean(centred * centred, axis=-1, keepdims=True) + norm_eps)
    standard = centred * inverse_dev
    return ((standard * norm_scale).astype(jnp.bfloat16), standard, inverse_dev)


def norm_backward(d_normed, d_output, standard, inverse_dev, norm_scale):
    scaled = d_normed * norm_scale
    inner = (
        scaled
        - jnp.mean(scaled, axis=-1, keepdims=True)
        - standard * jnp.mean(scaled * standard, axis=-1, keepdims=True)
    )
    return (d_output.astype(jnp.float32) + inner * inverse_dev).astype(jnp.bfloat16)


def softmax_rows(scores):
    lifted = jnp.exp(scores - jnp.max(scores, axis=-1, keepdims=True))
    return lifted / jnp.sum(lifted, axis=-1, keepdims=True)


def rounded(values):
    return lax.optimization_barrier(values.astype(jnp.bfloat16)).astype(jnp.float32)


def adam_update(gradient, master, first_moment, second_moment):
    new_first = beta_one * first_moment + (1.0 - beta_one) * gradient
    new_second = beta_two * second_moment + (1.0 - beta_two) * gradient * gradient
    direction = (
        new_first
        / (1.0 - beta_one**step_count)
        / (jnp.sqrt(new_second / (1.0 - beta_two**step_count)) + adam_eps)
    )
    new_master = master - learn_rate * (direction + decay_rate * master)
    return (new_master, new_first, new_second)


def layer_local(layer_in, norm_scale, weights):
    row_count, model_width = layer_in.shape
    col_count = weights.shape[1]
    head_count = col_count // HD
    length = row_count // MB_VOLS
    normed, standard, inverse_dev = norm_forward(layer_in, norm_scale)
    triple = weights[: 3 * model_width].reshape(3, model_width, col_count)
    project = jnp.einsum("nd,sdc->nsc", normed, triple, preferred_element_type=jnp.float32).astype(
        jnp.bfloat16
    )
    shaped = project.reshape(MB_VOLS, length, 3, head_count, HD)
    scores = jnp.einsum(
        "vqhe,vkhe->vhqk", shaped[:, :, 0], shaped[:, :, 1], preferred_element_type=jnp.float32
    ) * (1.0 / math.sqrt(HD))
    softmaxed = softmax_rows(scores)
    probs_half = softmaxed.astype(jnp.bfloat16)
    attended = jnp.einsum(
        "vhqk,vkhe->vqhe", probs_half, shaped[:, :, 2], preferred_element_type=jnp.float32
    )
    attended = attended.astype(jnp.bfloat16).reshape(row_count, col_count)
    return (normed, standard, inverse_dev, project, softmaxed, probs_half, attended)


def head_terms(attended, weights, model_width):
    return rounded(
        jnp.einsum(
            "nc,dc->nd", attended, weights[3 * model_width :], preferred_element_type=jnp.float32
        )
    )


def attention_back(d_output, saved_vals, weights):
    project, softmaxed, probs_half = (saved_vals[3], saved_vals[4], saved_vals[5])
    row_count, model_width = d_output.shape
    col_count = weights.shape[1]
    head_count = col_count // HD
    length = row_count // MB_VOLS
    shaped = project.reshape(MB_VOLS, length, 3, head_count, HD)
    d_attended = jnp.einsum(
        "nd,dc->nc", d_output, weights[3 * model_width :], preferred_element_type=jnp.float32
    )
    d_attended = d_attended.astype(jnp.bfloat16).reshape(MB_VOLS, length, head_count, HD)
    d_probs = jnp.einsum(
        "vqhe,vkhe->vhqk", d_attended, shaped[:, :, 2], preferred_element_type=jnp.float32
    )
    d_scores = (
        softmaxed
        * (d_probs - jnp.sum(d_probs * softmaxed, axis=-1, keepdims=True))
        * (1.0 / math.sqrt(HD))
    ).astype(jnp.bfloat16)
    d_queries = jnp.einsum(
        "vhqk,vkhe->vqhe", d_scores, shaped[:, :, 1], preferred_element_type=jnp.float32
    ).astype(jnp.bfloat16)
    d_keys = jnp.einsum(
        "vhqk,vqhe->vkhe", d_scores, shaped[:, :, 0], preferred_element_type=jnp.float32
    ).astype(jnp.bfloat16)
    d_values = jnp.einsum(
        "vhqk,vqhe->vkhe", probs_half, d_attended, preferred_element_type=jnp.float32
    ).astype(jnp.bfloat16)
    return jnp.stack([d_queries, d_keys, d_values], axis=2).reshape(row_count, 3, col_count)


def feature_terms(d_project, weights, model_width):
    col_count = weights.shape[1]
    triple = weights[: 3 * model_width].reshape(3, model_width, col_count)
    return rounded(jnp.einsum("nsc,sdc->nd", d_project, triple, preferred_element_type=jnp.float32))


def shards(
    patch_tokens, visible_index, output_grad, norm_gain, master_weights, first_moment, second_moment
):
    model_width = patch_tokens.shape[2] * lax.axis_size("mp")
    rows_here = master_weights.shape[1]
    is_first = lax.axis_index("segment") == 0
    norm_scale = norm_gain[0]
    weights = lax.all_gather(master_weights[0].astype(jnp.bfloat16), "dp", axis=0, tiled=True)
    tokens_full, grads_full = (
        lax.all_gather(patch_tokens, "mp", axis=2, tiled=True),
        lax.all_gather(output_grad, "mp", axis=2, tiled=True),
    )
    vol_count, length = visible_index.shape
    micro_count = vol_count // MB_VOLS
    mb_rows = MB_VOLS * length
    first_inputs = (
        tokens_full.astype(jnp.float32) + position_table(visible_index, model_width)
    ).astype(jnp.bfloat16)
    first_inputs = first_inputs.reshape(micro_count, mb_rows, model_width)
    out_grads = grads_full.reshape(micro_count, mb_rows, model_width)
    zeros_full = jnp.zeros((mb_rows, model_width), jnp.bfloat16)
    saved_ticks = []
    received = zeros_full
    for step_index in range(micro_count + 1):
        arriving = received
        own_input = first_inputs[step_index] if step_index < micro_count else zeros_full
        layer_in = jnp.where(is_first, own_input, arriving)
        saved_vals = layer_local(layer_in, norm_scale, weights)
        saved_ticks.append(saved_vals)
        if step_index < micro_count:
            head_part = head_terms(saved_vals[6], weights, model_width)
            mixed = lax.psum(head_part.astype(jnp.bfloat16), "mp").astype(jnp.float32)
            layer_out = (layer_in.astype(jnp.float32) + mixed).astype(jnp.bfloat16)
            received = from_behind(layer_out, "segment", 1)
    back_ticks = []
    for step_index in range(micro_count + 1):
        arriving = received if step_index > 0 else zeros_full
        own_grad = (
            out_grads[micro_count - 1 - step_index] if step_index < micro_count else zeros_full
        )
        d_output = jnp.where(is_first, arriving, own_grad)
        saved_vals = saved_ticks[micro_count - step_index]
        d_project = attention_back(d_output, saved_vals, weights)
        back_ticks.append((d_output, d_project))
        if step_index < micro_count:
            d_terms = feature_terms(d_project, weights, model_width)
            standard, inverse_dev = (saved_vals[1], saved_vals[2])
            summed = lax.psum(d_terms.astype(jnp.bfloat16), "mp").astype(jnp.float32)
            d_input = norm_backward(summed, d_output, standard, inverse_dev, norm_scale)
            received = from_behind(d_input, "segment", -1)
    all_steps = range(micro_count + 1)
    normed_ticks = jnp.stack([saved_ticks[micro_count - step_index][0] for step_index in all_steps])
    attended_ticks = jnp.stack(
        [saved_ticks[micro_count - step_index][6] for step_index in all_steps]
    )
    d_output_ticks = jnp.stack([back_ticks[step_index][0] for step_index in all_steps])
    d_project_ticks = jnp.stack([back_ticks[step_index][1] for step_index in all_steps])
    right_ticks = jnp.concatenate([d_project_ticks, attended_ticks[:, :, None]], axis=2)

    def pick_valid(ticks):
        chosen = jnp.where(is_first, ticks[1:], ticks[:-1])
        return chosen.reshape((micro_count * mb_rows,) + ticks.shape[2:])

    normed_all = pick_valid(normed_ticks)
    d_output_all = pick_valid(d_output_ticks)
    right_all = pick_valid(right_ticks)

    def one_piece(piece_index):
        first_row = piece_index * rows_here
        part_index = first_row // model_width
        col_offset = first_row % model_width
        left_norm = lax.dynamic_slice_in_dim(normed_all, col_offset, rows_here, 1)
        left_grad = lax.dynamic_slice_in_dim(d_output_all, col_offset, rows_here, 1)
        left_side = jnp.where(part_index == 3, left_grad, left_norm)
        right_side = lax.dynamic_index_in_dim(right_all, part_index, 1, keepdims=False)
        return jnp.einsum("tr,tc->rc", left_side, right_side, preferred_element_type=jnp.float32)

    blocks = lax.map(
        one_piece, jnp.arange(rows_here * lax.axis_size("dp") // rows_here, dtype=jnp.int32)
    )
    gradient = lax.psum_scatter(
        blocks.reshape(rows_here * lax.axis_size("dp"), blocks.shape[2]).astype(jnp.bfloat16),
        "dp",
        scatter_dimension=0,
        tiled=True,
    ).astype(jnp.float32)
    new_master, new_first, new_second = adam_update(
        gradient, master_weights[0], first_moment[0], second_moment[0]
    )
    return (new_master[None], new_first[None], new_second[None])


def solution(mesh):
    placed = (
        P("dp", None, "mp"),
        P("dp", None),
        P("dp", None, "mp"),
        P("segment", None),
        P("segment", "dp", "mp"),
        P("segment", "dp", "mp"),
        P("segment", "dp", "mp"),
    )
    return jax.shard_map(
        shards,
        mesh=mesh,
        in_specs=placed,
        out_specs=(P("segment", "dp", "mp"), P("segment", "dp", "mp"), P("segment", "dp", "mp")),
        check_vma=False,
    )
```

profile of v0, /device:TPU:0, one launch (start us, length us, event | category | flops | bytes accessed | tf_op | source)
XLA Modules:
  0.0 909.8 jit_solution(2568975783798834956)
XLA Ops:
  7.2 4.9 bitcast_convert_fusion
  12.3 10.1 %all_gather.10 = bf16[8,16,3072]{2,1,0:T(8,128)(2,1)S(1)} all-gather(bf16[8,16,768]{2,1,0:T(8,128)(2,1)S(1)} %copy-done.3), channel_id=1, replica_groups=mesh['segment'=2,'dp'=4,'mp'=4] {'mp'}, dimensions={2}, use_global_device_ids=true | all-gather | bytes 983040 | tf_op jit(solution)/shard_map/all_gather | solution.py:149
  22.3 2.8 multiply_sine_fusion
  25.8 207.5 %all-gather.2.cloned.1.call-done = bf16[12288,512]{1,0:T(8,128)(2,1)} async-done(((bf16[3072,512]{1,0:T(8,128)(2,1)}), bf16[12288,512]{1,0:T(8,128)(2,1)}) %all-gather.2.cloned.1.call-update) | async-done | bytes 12582928 | tf_op jit(solution)/shard_map/all_gather | solution.py:147
  233.2 5.2 slice.160
  238.5 3.6 copy-done
  244.9 3.6 convolution_convert_fusion.3
  248.6 30.0 %all-reduce.9.cloned.1.call-done = bf16[32,3072]{1,0:T(8,128)(2,1)} async-done(((bf16[32,3072]{1,0:T(8,128)(2,1)}), bf16[32,3072]{1,0:T(8,128)(2,1)}) %all-reduce.9.cloned.1.call-update) | async-done | bytes 196624 | tf_op jit(solution)/shard_map/psum | solution.py:171
  279.6 3.4 collective-permute-start
  283.0 3.1 collective-permute-done
  286.6 5.5 convolution_convert_fusion.7
  293.3 3.6 convolution_convert_fusion.2
  297.0 33.0 %all-reduce.11.cloned.1.call-done = bf16[32,3072]{1,0:T(8,128)(2,1)} async-done(((bf16[32,3072]{1,0:T(8,128)(2,1)}), bf16[32,3072]{1,0:T(8,128)(2,1)}) %all-reduce.11.cloned.1.call-update) | async-done | bytes 196624 | tf_op jit(solution)/shard_map/psum | solution.py:171
  330.9 3.4 collective-permute-start.1
  334.3 3.2 collective-permute-done.1
  337.9 5.5 convolution_convert_fusion.6
  344.7 3.6 convolution_convert_fusion.1
  348.4 7.8 all_gather.9
  356.2 25.1 %all-reduce.13.cloned.1.call-done = bf16[32,3072]{1,0:T(8,128)(2,1)} async-done(((bf16[32,3072]{1,0:T(8,128)(2,1)}), bf16[32,3072]{1,0:T(8,128)(2,1)}) %all-reduce.13.cloned.1.call-update) | async-done | bytes 196624 | tf_op jit(solution)/shard_map/psum | solution.py:171
  382.3 3.6 collective-permute-start.2
  386.1 2.8 collective-permute-done.2
  389.3 5.5 convolution_convert_fusion.5
  395.4 3.6 convolution_convert_fusion
  399.8 32.2 %all-reduce.15.cloned.1.call-done = bf16[32,3072]{1,0:T(8,128)(2,1)} async-done(((bf16[32,3072]{1,0:T(8,128)(2,1)}), bf16[32,3072]{1,0:T(8,128)(2,1)}) %all-reduce.15.cloned.1.call-update) | async-done | bytes 196624 | tf_op jit(solution)/shard_map/psum | solution.py:171
  433.0 3.4 collective-permute-start.3
  440.0 5.5 convolution_convert_fusion.4
  446.7 7.2 fusion.21
  456.2 30.7 %all-reduce.17.cloned.1.call-done = bf16[32,3072]{1,0:T(8,128)(2,1)} async-done(((bf16[32,3072]{1,0:T(8,128)(2,1)}), bf16[32,3072]{1,0:T(8,128)(2,1)}) %all-reduce.17.cloned.1.call-update) | async-done | bytes 196624 | tf_op jit(solution)/shard_map/psum | solution.py:187
  490.5 6.2 collective-permute-done.4
  496.8 2.5 convolution_convert_fusion.12
  500.4 7.2 fusion.22
  507.7 31.0 %all-reduce.19.cloned.1.call-done = bf16[32,3072]{1,0:T(8,128)(2,1)} async-done(((bf16[32,3072]{1,0:T(8,128)(2,1)}), bf16[32,3072]{1,0:T(8,128)(2,1)}) %all-reduce.19.cloned.1.call-update) | async-done | bytes 196624 | tf_op jit(solution)/shard_map/psum | solution.py:187
  542.4 6.2 collective-permute-done.5
  548.7 2.5 convolution_convert_fusion.11
  552.2 7.2 fusion.23
  559.6 30.9 %all-reduce.21.cloned.1.call-done = bf16[32,3072]{1,0:T(8,128)(2,1)} async-done(((bf16[32,3072]{1,0:T(8,128)(2,1)}), bf16[32,3072]{1,0:T(8,128)(2,1)}) %all-reduce.21.cloned.1.call-update) | async-done | bytes 196624 | tf_op jit(solution)/shard_map/psum | solution.py:187
  594.5 5.9 collective-permute-done.6
  600.5 2.5 convolution_convert_fusion.10
  604.1 7.2 fusion.24
  611.4 31.0 %all-reduce.23.cloned.1.call-done = bf16[32,3072]{1,0:T(8,128)(2,1)} async-done(((bf16[32,3072]{1,0:T(8,128)(2,1)}), bf16[32,3072]{1,0:T(8,128)(2,1)}) %all-reduce.23.cloned.1.call-update) | async-done | bytes 196624 | tf_op jit(solution)/shard_map/psum | solution.py:187
  646.3 6.1 collective-permute-done.7
  659.7 15.8 %while.12 = (s32[]{:T(128)}, bf16[4,3072,512]{2,1,0:T(8,128)(2,1)}, s32[4]{0:T(128)S(1)}, bf16[128,3072]{1,0:T(8,128)(2,1)S(1)}, bf16[128,3072]{1,0:T(8,128)(2,1...) while((s32[]{:T(128)}, bf16[4,3072,512]{2,1,0:T(8,128)(2,1)}, ...), condition=%wide.region_42.43_spmd, body=%wide.region_41.42_spmd.sunk | while | flops 403046400 | bytes 7996187 | solution.py:217
  661.0 2.7 bitcast_dynamic-update-slice_fusion.2
  664.9 2.7 bitcast_dynamic-update-slice_fusion.2
  668.8 2.7 bitcast_dynamic-update-slice_fusion.2
  672.8 2.7 bitcast_dynamic-update-slice_fusion.2
  675.5 211.3 %reduce-scatter.2.cloned.1.call-done = bf16[3072,512]{1,0:T(8,128)(2,1)} async-done(((bf16[12288,512]{1,0:T(8,128)(2,1)}), bf16[3072,512]{1,0:T(8,128)(2,1)}) %reduce-scatter.2.cloned.1.call-update) | async-done | bytes 3145744 | tf_op jit(solution)/shard_map/reduce_scatter | solution.py:220
  886.8 16.1 %fusion.25 = (f32[1,3072,512]{2,1,0:T(8,128)}, f32[1,3072,512]{2,1,0:T(8,128)}, f32[1,3072,512]{2,1,0:T(8,128)}) fusion(bf16[3072,512]{1,0:T(8,128)(2,1)} %reduce-scatter.2.cloned.1.call-done, f32[1,3072,512]{2,1,0:T(8,128)} %param.15, f32[1,3072,512]{2,1,0:T(8,128)} %param.14, f32[1,3072,512]{2,1,0:T(8,128)} %param.13), kind=kLoop, calls=%fused_computation.39 | loop fusion | flops 25165824 | bytes 40894464 | tf_op jit(solution)/shard_map/broadcast_in_dim | solution.py:229
  (268 shorter events, 47.9 us)
Async XLA Ops:
  7.2 5.1 copy-start.3
  7.2 226.1 %all-gather.2.cloned.1.call-start = ((), (), s32[]{:S(2)}) async-start(), calls=%async_computation.1 | async-start | bytes 15728640 | tf_op jit(solution)/shard_map/all_gather | solution.py:147
  12.1 13.5 %copy-start.1 = (f32[1,3072]{1,0:T(1,128)S(1)}, f32[1,3072]{1,0:T(1,128)}, u32[]{:S(2)}) copy-start(f32[1,3072]{1,0:T(1,128)} %param.12) | copy-start | bytes 36868
  12.2 266.4 %all-reduce.9.cloned.1.call-start = ((), (), s32[]{:S(2)}) async-start(), calls=%async_computation.2 | async-start | bytes 393216 | tf_op jit(solution)/shard_map/psum | solution.py:171
  243.7 34.8 %copy-start.17 = (bf16[2,16,1,4,128]{4,3,1,0,2:T(4,128)(2,1)}, bf16[2,16,1,4,128]{4,3,1,0,2:T(4,128)(2,1)S(1)}, u32[]{:S(2)}) copy-start(bf16[2,16,1,4,128]{4,3,1,0,2:T(4,128)(2,1)S(1)} %get-tuple-element.136) | copy-start | bytes 98308
  243.7 35.8 %copy-start.9 = (bf16[2,16,1,4,128]{4,3,1,0,2:T(4,128)(2,1)}, bf16[2,16,1,4,128]{4,3,1,0,2:T(4,128)(2,1)S(1)}, u32[]{:S(2)}) copy-start(bf16[2,16,1,4,128]{4,3,1,0,2:T(4,128)(2,1)S(1)} %get-tuple-element.137) | copy-start | bytes 98308
  243.8 35.8 %copy-start.15 = (bf16[2,16,1,4,128]{4,3,1,0,2:T(4,128)(2,1)}, bf16[2,16,1,4,128]{4,3,1,0,2:T(4,128)(2,1)S(1)}, u32[]{:S(2)}) copy-start(bf16[2,16,1,4,128]{4,3,1,0,2:T(4,128)(2,1)S(1)} %get-tuple-element.135) | copy-start | bytes 98308
  244.6 35.0 %copy-start.30 = (f32[2,4,16]{2,1,0:T(4,128)}, f32[2,4,16]{2,1,0:T(4,128)S(1)}, u32[]{:S(2)}) copy-start(f32[2,4,16]{2,1,0:T(4,128)S(1)} %get-tuple-element.140) | copy-start | bytes 1540
  248.5 81.4 %all-reduce.11.cloned.1.call-start = ((), (), s32[]{:S(2)}) async-start(), calls=%async_computation.3 | async-start | bytes 393216 | tf_op jit(solution)/shard_map/psum | solution.py:171
  279.6 6.6 collective-permute-start
  292.1 37.8 %copy-start.21 = (bf16[2,16,1,4,128]{4,3,1,0,2:T(4,128)(2,1)}, bf16[2,16,1,4,128]{4,3,1,0,2:T(4,128)(2,1)S(1)}, u32[]{:S(2)}) copy-start(bf16[2,16,1,4,128]{4,3,1,0,2:T(4,128)(2,1)S(1)} %get-tuple-element.133) | copy-start | bytes 98308
  292.9 44.7 %copy-start.32 = (f32[2,4,16]{2,1,0:T(4,128)}, f32[2,4,16]{2,1,0:T(4,128)S(1)}, u32[]{:S(2)}) copy-start(f32[2,4,16]{2,1,0:T(4,128)S(1)} %get-tuple-element.142) | copy-start | bytes 1540
  296.9 84.4 %all-reduce.13.cloned.1.call-start = ((), (), s32[]{:S(2)}) async-start(), calls=%async_computation.4 | async-start | bytes 393216 | tf_op jit(solution)/shard_map/psum | solution.py:171
  330.9 6.6 collective-permute-start.1
  337.9 10.4 %copy-start.4 = (bf16[8,16,768]{2,1,0:T(8,128)(2,1)S(1)}, bf16[8,16,768]{2,1,0:T(8,128)(2,1)}, u32[]{:S(2)}) copy-start(bf16[8,16,768]{2,1,0:T(8,128)(2,1)} %param.11) | copy-start | bytes 589828
  343.5 38.8 %copy-start.23 = (bf16[2,16,1,4,128]{4,3,1,0,2:T(4,128)(2,1)}, bf16[2,16,1,4,128]{4,3,1,0,2:T(4,128)(2,1)S(1)}, u32[]{:S(2)}) copy-start(bf16[2,16,1,4,128]{4,3,1,0,2:T(4,128)(2,1)S(1)} %get-tuple-element.129) | copy-start | bytes 98308
  343.5 38.8 %copy-start.25 = (bf16[2,16,1,4,128]{4,3,1,0,2:T(4,128)(2,1)}, bf16[2,16,1,4,128]{4,3,1,0,2:T(4,128)(2,1)S(1)}, u32[]{:S(2)}) copy-start(bf16[2,16,1,4,128]{4,3,1,0,2:T(4,128)(2,1)S(1)} %get-tuple-element.130) | copy-start | bytes 98308
  344.3 38.0 %copy-start.34 = (f32[2,4,16]{2,1,0:T(4,128)}, f32[2,4,16]{2,1,0:T(4,128)S(1)}, u32[]{:S(2)}) copy-start(f32[2,4,16]{2,1,0:T(4,128)S(1)} %get-tuple-element.144) | copy-start | bytes 1540
  348.3 83.8 %all-reduce.15.cloned.1.call-start = ((), (), s32[]{:S(2)}) async-start(), calls=%async_computation.5 | async-start | bytes 393216 | tf_op jit(solution)/shard_map/psum | solution.py:171
  382.3 6.6 collective-permute-start.2
  399.0 87.9 %all-reduce.17.cloned.1.call-start = ((), (), s32[]{:S(2)}) async-start(), calls=%async_computation.6 | async-start | bytes 393216 | tf_op jit(solution)/shard_map/psum | solution.py:187
  433.0 6.6 collective-permute-start.3
  453.9 84.9 %all-reduce.19.cloned.1.call-start = ((), (), s32[]{:S(2)}) async-start(), calls=%async_computation.7 | async-start | bytes 393216 | tf_op jit(solution)/shard_map/psum | solution.py:187
  489.2 7.6 collective-permute-start.4
  500.3 42.1 %copy-start.6 = (bf16[1,32,1,512]{3,1,2,0:T(8,128)(2,1)S(1)}, bf16[1,32,1,512]{3,1,2,0:T(8,128)(2,1)}, u32[]{:S(2)}) copy-start(bf16[1,32,1,512]{3,1,2,0:T(8,128)(2,1)} %stack.162) | copy-start | bytes 98308
  500.3 42.1 %copy-start.7 = (bf16[1,32,1,512]{3,1,2,0:T(8,128)(2,1)S(1)}, bf16[1,32,1,512]{3,1,2,0:T(8,128)(2,1)}, u32[]{:S(2)}) copy-start(bf16[1,32,1,512]{3,1,2,0:T(8,128)(2,1)} %stack.163) | copy-start | bytes 98308
  500.3 42.1 %copy-start.8 = (bf16[1,32,1,512]{3,1,2,0:T(8,128)(2,1)S(1)}, bf16[1,32,1,512]{3,1,2,0:T(8,128)(2,1)}, u32[]{:S(2)}) copy-start(bf16[1,32,1,512]{3,1,2,0:T(8,128)(2,1)} %stack.164) | copy-start | bytes 98308
  500.4 50.9 %copy-start.14 = (bf16[2,16,1,4,128]{4,3,1,0,2:T(4,128)(2,1)S(1)}, bf16[2,16,1,4,128]{4,3,1,0,2:T(4,128)(2,1)}, u32[]{:S(2)}) copy-start(bf16[2,16,1,4,128]{4,3,1,0,2:T(4,128)(2,1)} %copy-done.13) | copy-start | bytes 98308
  500.4 51.0 %copy-start.24 = (bf16[2,16,1,4,128]{4,3,1,0,2:T(4,128)(2,1)S(1)}, bf16[2,16,1,4,128]{4,3,1,0,2:T(4,128)(2,1)}, u32[]{:S(2)}) copy-start(bf16[2,16,1,4,128]{4,3,1,0,2:T(4,128)(2,1)} %copy-done.23) | copy-start | bytes 98308
  500.4 51.0 %copy-start.29 = (f32[2,4,16,16]{2,3,1,0:T(8,128)S(1)}, f32[2,4,16,16]{2,3,1,0:T(8,128)}, u32[]{:S(2)}) copy-start(f32[2,4,16,16]{2,3,1,0:T(8,128)} %get-tuple-element.145) | copy-start | bytes 24580
  500.4 51.0 %copy-start.35 = (f32[2,4,16]{2,1,0:T(4,128)S(1)}, f32[2,4,16]{2,1,0:T(4,128)}, u32[]{:S(2)}) copy-start(f32[2,4,16]{2,1,0:T(4,128)} %copy-done.34) | copy-start | bytes 1540
  507.6 44.0 %copy-start.26 = (bf16[2,16,1,4,128]{4,3,1,0,2:T(4,128)(2,1)S(1)}, bf16[2,16,1,4,128]{4,3,1,0,2:T(4,128)(2,1)}, u32[]{:S(2)}) copy-start(bf16[2,16,1,4,128]{4,3,1,0,2:T(4,128)(2,1)} %copy-done.25) | copy-start | bytes 98308
  507.7 82.9 %all-reduce.21.cloned.1.call-start = ((), (), s32[]{:S(2)}) async-start(), calls=%async_computation.8 | async-start | bytes 393216 | tf_op jit(solution)/shard_map/psum | solution.py:187
  541.1 7.6 collective-permute-start.5
  552.2 7.3 copy-start.5
  559.4 43.6 %copy-start.12 = (bf16[2,16,1,4,128]{4,3,1,0,2:T(4,128)(2,1)S(1)}, bf16[2,16,1,4,128]{4,3,1,0,2:T(4,128)(2,1)}, u32[]{:S(2)}) copy-start(bf16[2,16,1,4,128]{4,3,1,0,2:T(4,128)(2,1)} %copy-done.11) | copy-start | bytes 98308
  559.4 43.8 %copy-start.20 = (bf16[2,16,1,4,128]{4,3,1,0,2:T(4,128)(2,1)S(1)}, bf16[2,16,1,4,128]{4,3,1,0,2:T(4,128)(2,1)}, u32[]{:S(2)}) copy-start(bf16[2,16,1,4,128]{4,3,1,0,2:T(4,128)(2,1)} %copy-done.19) | copy-start | bytes 98308
  559.4 43.8 %copy-start.28 = (f32[2,4,16,16]{2,3,1,0:T(8,128)S(1)}, f32[2,4,16,16]{2,3,1,0:T(8,128)}, u32[]{:S(2)}) copy-start(f32[2,4,16,16]{2,3,1,0:T(8,128)} %get-tuple-element.143) | copy-start | bytes 24580
  559.4 43.8 %copy-start.33 = (f32[2,4,16]{2,1,0:T(4,128)S(1)}, f32[2,4,16]{2,1,0:T(4,128)}, u32[]{:S(2)}) copy-start(f32[2,4,16]{2,1,0:T(4,128)} %copy-done.32) | copy-start | bytes 1540
  559.4 44.0 %copy-start.22 = (bf16[2,16,1,4,128]{4,3,1,0,2:T(4,128)(2,1)S(1)}, bf16[2,16,1,4,128]{4,3,1,0,2:T(4,128)(2,1)}, u32[]{:S(2)}) copy-start(bf16[2,16,1,4,128]{4,3,1,0,2:T(4,128)(2,1)} %copy-done.21) | copy-start | bytes 98308
  559.5 83.0 %all-reduce.23.cloned.1.call-start = ((), (), s32[]{:S(2)}) async-start(), calls=%async_computation.9 | async-start | bytes 393216 | tf_op jit(solution)/shard_map/psum | solution.py:187
  592.9 7.6 collective-permute-start.6
  611.3 44.3 %copy-start.10 = (bf16[2,16,1,4,128]{4,3,1,0,2:T(4,128)(2,1)S(1)}, bf16[2,16,1,4,128]{4,3,1,0,2:T(4,128)(2,1)}, u32[]{:S(2)}) copy-start(bf16[2,16,1,4,128]{4,3,1,0,2:T(4,128)(2,1)} %copy-done.9) | copy-start | bytes 98308
  611.3 44.4 %copy-start.16 = (bf16[2,16,1,4,128]{4,3,1,0,2:T(4,128)(2,1)S(1)}, bf16[2,16,1,4,128]{4,3,1,0,2:T(4,128)(2,1)}, u32[]{:S(2)}) copy-start(bf16[2,16,1,4,128]{4,3,1,0,2:T(4,128)(2,1)} %copy-done.15) | copy-start | bytes 98308
  611.3 44.4 %copy-start.31 = (f32[2,4,16]{2,1,0:T(4,128)S(1)}, f32[2,4,16]{2,1,0:T(4,128)}, u32[]{:S(2)}) copy-start(f32[2,4,16]{2,1,0:T(4,128)} %copy-done.30) | copy-start | bytes 1540
  611.3 45.6 %copy-start.18 = (bf16[2,16,1,4,128]{4,3,1,0,2:T(4,128)(2,1)S(1)}, bf16[2,16,1,4,128]{4,3,1,0,2:T(4,128)(2,1)}, u32[]{:S(2)}) copy-start(bf16[2,16,1,4,128]{4,3,1,0,2:T(4,128)(2,1)} %copy-done.17) | copy-start | bytes 98308
  611.3 275.4 %reduce-scatter.2.cloned.1.call-start = ((), (), s32[]{:S(2)}) async-start(), calls=%async_computation.10 | async-start | bytes 15728640 | tf_op jit(solution)/shard_map/reduce_scatter | solution.py:220
  644.8 7.6 collective-permute-start.7
  (6 other events, 19.8 us)
Sparse Core Ops, SparseCore 0:
  12.3 220.9 all-gather.1
  248.7 29.8 all-reduce.8
  297.0 32.8 all-reduce.10
  348.4 32.8 all-reduce.12
  399.1 32.8 all-reduce.14
  454.0 32.8 all-reduce.16
  507.8 30.9 all-reduce.18
  559.6 30.9 all-reduce.20
  611.5 30.9 all-reduce.22
  675.6 211.1 reduce-scatter.1
where the time goes:
time: 911 us; the launch traced here: 910 us
  waiting for transfers between devices  697 us (77%)
  matrix products  100 us (11%)
  other arithmetic  41.1 us (5%)
  starting transfers between devices  19.5 us (2%)
  blocking collectives  17.9 us (2%)
  local copies, waits for them, and re-layouts  16 us (2%)
  between operations  15.4 us (2%)
    reduce_scatter x1, waiting for transfers between devices, shards(): lax.psum_scatter(blocks.reshape(rows_here * lax.axis_size('dp'), blocks.s...  211 us
    all_gather x1, waiting for transfers between devices, shards(): lax.all_gather(master_weights[0].astype(jnp.bfloat16), 'dp', axis=0, tile...  207 us
    psum x4, waiting for transfers between devices, shards(): summed = lax.psum(d_terms.astype(jnp.bfloat16), 'mp').astype(jnp.float32)  124 us
    psum x4, waiting for transfers between devices, shards(): mixed = lax.psum(head_part.astype(jnp.bfloat16), 'mp').astype(jnp.float32)  120 us
    ppermute x8, waiting for transfers between devices, from_behind(): return lax.ppermute(array, axis, pairs)  34 us
    dot_general x4, matrix products, feature_terms(): jnp.einsum('nsc,sdc->nd', d_project, triple, preferred_element_type=jnp.f...  28.8 us
    dot_general x5, matrix products, layer_local(): jnp.einsum('nd,sdc->nsc', normed, triple, preferred_element_type=jnp.floa...  23.5 us
    ppermute x8, starting transfers between devices, from_behind(): return lax.ppermute(array, axis, pairs)  19.1 us
  transfers between devices with their start and end apart: 18, of which 18 were waited for; matrix products, arithmetic and copies ran while one was open for 1% of the time, Pallas kernels for 0%

commit v1 on v0

--- a/solution.py
+++ b/solution.py
@@ -168,7 +168,9 @@
         saved_ticks.append(saved_vals)
         if step_index < micro_count:
             head_part = head_terms(saved_vals[6], weights, model_width)
-            mixed = lax.psum(head_part.astype(jnp.bfloat16), "mp").astype(jnp.float32)
+            mixed = jnp.sum(lax.all_gather(head_part.astype(jnp.bfloat16), "mp"), axis=0).astype(
+                jnp.float32
+            )
             layer_out = (layer_in.astype(jnp.float32) + mixed).astype(jnp.bfloat16)
             received = from_behind(layer_out, "segment", 1)
     back_ticks = []

time: 911 us -> 818 us (0.90)
  waiting for transfers between devices: 697 us -> 574 us
  blocking collectives: 17.9 us -> 52.3 us
    psum x4 -> x0, waiting for transfers between devices: 120 us -> none  [shards(): mixed = lax.psum(head_part.astype(jnp.bfloat16), 'mp').astype(jnp.float32)]
    all_gather x0 -> x4, blocking collectives: none -> 33.8 us  [shards(): lax.all_gather(head_part.astype(jnp.bfloat16), 'mp')]
  transfers between devices with their start and end apart: 18 -> 14, of which waited for: 18 -> 13; matrix products, arithmetic and copies ran while one was open for 1% -> 1% of each run, Pallas kernels for 0% -> 0%
where the time goes in v1:
time: 818 us; the launch traced here: 817 us
  waiting for transfers between devices  574 us (70%)
  matrix products  96.2 us (12%)
  blocking collectives  52.3 us (6%)
  other arithmetic  41.5 us (5%)
  starting transfers between devices  19.4 us (2%)
  between operations  15.4 us (2%)
  local copies, waits for them, and re-layouts  14.9 us (2%)
    reduce_scatter x1, waiting for transfers between devices, shards(): lax.psum_scatter(blocks.reshape(rows_here * lax.axis_size('dp'), blocks.s...  211 us
    all_gather x1, waiting for transfers between devices, shards(): lax.all_gather(master_weights[0].astype(jnp.bfloat16), 'dp', axis=0, tile...  207 us
    psum x4, waiting for transfers between devices, shards(): summed = lax.psum(d_terms.astype(jnp.bfloat16), 'mp').astype(jnp.float32)  123 us
    all_gather x4, blocking collectives, shards(): lax.all_gather(head_part.astype(jnp.bfloat16), 'mp')  33.8 us
    ppermute x8, waiting for transfers between devices, from_behind(): return lax.ppermute(array, axis, pairs)  32.9 us
    dot_general x4, matrix products, feature_terms(): jnp.einsum('nsc,sdc->nd', d_project, triple, preferred_element_type=jnp.f...  28.9 us
    dot_general x5, matrix products, layer_local(): jnp.einsum('nd,sdc->nsc', normed, triple, preferred_element_type=jnp.floa...  23.4 us
    ppermute x8, starting transfers between devices, from_behind(): return lax.ppermute(array, axis, pairs)  19.1 us
  transfers between devices with their start and end apart: 14, of which 13 were waited for; matrix products, arithmetic and copies ran while one was open for 1% of the time, Pallas kernels for 0%

profile of v1, /device:TPU:0, one launch (start us, length us, event | category | flops | bytes accessed | tf_op | source)
XLA Modules:
  0.0 816.7 jit_solution(10002770978799164355)
XLA Ops:
  7.2 4.9 bitcast_convert_fusion
  12.3 10.1 %all_gather.34 = bf16[8,16,3072]{2,1,0:T(8,128)(2,1)S(1)} all-gather(bf16[8,16,768]{2,1,0:T(8,128)(2,1)S(1)} %copy-done.6), channel_id=1, replica_groups=mesh['segment'=2,'dp'=4,'mp'=4] {'mp'}, dimensions={2}, use_global_device_ids=true | all-gather | bytes 983040 | tf_op jit(solution)/shard_map/all_gather | solution.py:149
  22.3 2.8 multiply_sine_fusion
  26.5 206.7 %all-gather.6.cloned.1.call-done = bf16[12288,512]{1,0:T(8,128)(2,1)} async-done(((bf16[3072,512]{1,0:T(8,128)(2,1)}), bf16[12288,512]{1,0:T(8,128)(2,1)}) %all-gather.6.cloned.1.call-update) | async-done | bytes 12582928 | tf_op jit(solution)/shard_map/all_gather | solution.py:147
  233.2 5.2 slice.160
  238.5 3.6 copy-done
  244.9 2.9 convolution_convert_fusion.3
  247.8 8.5 %all-gather = bf16[128,3072]{1,0:T(8,128)(2,1)S(1)} all-gather(bf16[32,3072]{1,0:T(8,128)(2,1)S(1)} %convolution_convert_fusion.3), channel_id=2, replica_groups=mesh['segment'=2,'dp'=4,'mp'=4] {'mp'}, dimensions={0}, use_global_device_ids=true | all-gather | bytes 983040 | tf_op jit(solution)/shard_map/all_gather | solution.py:171
  256.6 3.4 collective-permute-start
  260.0 8.4 %all_gather.33 = bf16[8,16,3072]{2,1,0:T(8,128)(2,1)S(1)} all-gather(bf16[8,16,768]{2,1,0:T(8,128)(2,1)S(1)} %copy-done.7), channel_id=1, replica_groups=mesh['segment'=2,'dp'=4,'mp'=4] {'mp'}, dimensions={2}, use_global_device_ids=true | all-gather | bytes 983040 | tf_op jit(solution)/shard_map/all_gather | solution.py:150
  268.9 5.5 convolution_convert_fusion.7
  275.7 2.9 convolution_convert_fusion.2
  278.6 8.7 %all-gather.1 = bf16[128,3072]{1,0:T(8,128)(2,1)S(1)} all-gather(bf16[32,3072]{1,0:T(8,128)(2,1)S(1)} %convolution_convert_fusion.2), channel_id=3, replica_groups=mesh['segment'=2,'dp'=4,'mp'=4] {'mp'}, dimensions={0}, use_global_device_ids=true | all-gather | bytes 983040 | tf_op jit(solution)/shard_map/all_gather | solution.py:171
  289.3 4.4 collective-permute-done.1
  295.1 5.5 convolution_convert_fusion.6
  301.9 2.9 convolution_convert_fusion.1
  304.8 8.6 %all-gather.2 = bf16[128,3072]{1,0:T(8,128)(2,1)S(1)} all-gather(bf16[32,3072]{1,0:T(8,128)(2,1)S(1)} %convolution_convert_fusion.1), channel_id=4, replica_groups=mesh['segment'=2,'dp'=4,'mp'=4] {'mp'}, dimensions={0}, use_global_device_ids=true | all-gather | bytes 983040 | tf_op jit(solution)/shard_map/all_gather | solution.py:171
  313.6 4.4 collective-permute-start.2
  318.8 3.9 collective-permute-done.2
  323.1 5.5 convolution_convert_fusion.5
  330.4 2.9 convolution_convert_fusion
  333.3 7.9 all-gather.3
  341.5 4.4 collective-permute-start.3
  345.9 2.5 convolution_convert_fusion.13
  350.9 5.5 convolution_convert_fusion.4
  357.6 7.2 fusion.21
  365.4 30.2 %all-reduce.5.cloned.1.call-done = bf16[32,3072]{1,0:T(8,128)(2,1)} async-done(((bf16[32,3072]{1,0:T(8,128)(2,1)}), bf16[32,3072]{1,0:T(8,128)(2,1)}) %all-reduce.5.cloned.1.call-update) | async-done | bytes 196624 | tf_op jit(solution)/shard_map/psum | solution.py:189
  399.2 6.2 collective-permute-done.4
  405.5 2.5 convolution_convert_fusion.12
  409.1 7.2 fusion.22
  416.4 31.0 %all-reduce.7.cloned.1.call-done = bf16[32,3072]{1,0:T(8,128)(2,1)} async-done(((bf16[32,3072]{1,0:T(8,128)(2,1)}), bf16[32,3072]{1,0:T(8,128)(2,1)}) %all-reduce.7.cloned.1.call-update) | async-done | bytes 196624 | tf_op jit(solution)/shard_map/psum | solution.py:189
  451.7 5.6 collective-permute-done.5
  457.4 2.5 convolution_convert_fusion.11
  460.9 7.2 fusion.23
  468.3 30.9 %all-reduce.9.cloned.1.call-done = bf16[32,3072]{1,0:T(8,128)(2,1)} async-done(((bf16[32,3072]{1,0:T(8,128)(2,1)}), bf16[32,3072]{1,0:T(8,128)(2,1)}) %all-reduce.9.cloned.1.call-update) | async-done | bytes 196624 | tf_op jit(solution)/shard_map/psum | solution.py:189
  504.5 4.7 collective-permute-done.6
  509.2 2.5 convolution_convert_fusion.10
  512.8 7.3 fusion.24
  520.2 31.0 %all-reduce.11.cloned.1.call-done = bf16[32,3072]{1,0:T(8,128)(2,1)} async-done(((bf16[32,3072]{1,0:T(8,128)(2,1)}), bf16[32,3072]{1,0:T(8,128)(2,1)}) %all-reduce.11.cloned.1.call-update) | async-done | bytes 196624 | tf_op jit(solution)/shard_map/psum | solution.py:189
  555.0 6.1 collective-permute-done.7
  561.8 2.5 convolution_convert_fusion.9
  566.6 15.8 %while.12 = (s32[]{:T(128)}, bf16[4,3072,512]{2,1,0:T(8,128)(2,1)}, s32[4]{0:T(128)S(1)}, bf16[128,3072]{1,0:T(8,128)(2,1)S(1)}, bf16[128,3072]{1,0:T(8,128)(2,1...) while((s32[]{:T(128)}, bf16[4,3072,512]{2,1,0:T(8,128)(2,1)}, ...), condition=%wide.region_42.43_spmd, body=%wide.region_41.42_spmd.sunk | while | flops 403046400 | bytes 7996187 | solution.py:219
  567.9 2.7 bitcast_dynamic-update-slice_fusion.2
  571.8 2.7 bitcast_dynamic-update-slice_fusion.2
  575.8 2.7 bitcast_dynamic-update-slice_fusion.2
  579.7 2.7 bitcast_dynamic-update-slice_fusion.2
  582.4 211.3 %reduce-scatter.2.cloned.1.call-done = bf16[3072,512]{1,0:T(8,128)(2,1)} async-done(((bf16[12288,512]{1,0:T(8,128)(2,1)}), bf16[3072,512]{1,0:T(8,128)(2,1)}) %reduce-scatter.2.cloned.1.call-update) | async-done | bytes 3145744 | tf_op jit(solution)/shard_map/reduce_scatter | solution.py:222
  793.7 16.1 %fusion.25 = (f32[1,3072,512]{2,1,0:T(8,128)}, f32[1,3072,512]{2,1,0:T(8,128)}, f32[1,3072,512]{2,1,0:T(8,128)}) fusion(bf16[3072,512]{1,0:T(8,128)(2,1)} %reduce-scatter.2.cloned.1.call-done, f32[1,3072,512]{2,1,0:T(8,128)} %param.15, f32[1,3072,512]{2,1,0:T(8,128)} %param.14, f32[1,3072,512]{2,1,0:T(8,128)} %param.13), kind=kLoop, calls=%fused_computation.39 | loop fusion | flops 25165824 | bytes 40894464 | tf_op jit(solution)/shard_map/broadcast_in_dim | solution.py:231
  (284 shorter events, 43.7 us)
Async XLA Ops:
  7.2 226.1 %all-gather.6.cloned.1.call-start = ((), (), s32[]{:S(2)}) async-start(), calls=%async_computation.1 | async-start | bytes 15728640 | tf_op jit(solution)/shard_map/all_gather | solution.py:147
  12.1 13.5 %copy-start.1 = (f32[1,3072]{1,0:T(1,128)S(1)}, f32[1,3072]{1,0:T(1,128)}, u32[]{:S(2)}) copy-start(f32[1,3072]{1,0:T(1,128)} %param.12) | copy-start | bytes 36868
  12.2 383.4 %all-reduce.5.cloned.1.call-start = ((), (), s32[]{:S(2)}) async-start(), calls=%async_computation.2 | async-start | bytes 393216 | tf_op jit(solution)/shard_map/psum | solution.py:189
  242.0 18.0 %copy-start.7 = (bf16[8,16,768]{2,1,0:T(8,128)(2,1)S(1)}, bf16[8,16,768]{2,1,0:T(8,128)(2,1)}, u32[]{:S(2)}) copy-start(bf16[8,16,768]{2,1,0:T(8,128)(2,1)} %param.11) | copy-start | bytes 589828
  243.7 30.6 %copy-start.9 = (bf16[2,16,1,4,128]{4,3,1,0,2:T(4,128)(2,1)}, bf16[2,16,1,4,128]{4,3,1,0,2:T(4,128)(2,1)S(1)}, u32[]{:S(2)}) copy-start(bf16[2,16,1,4,128]{4,3,1,0,2:T(4,128)(2,1)S(1)} %get-tuple-element.137) | copy-start | bytes 98308
  243.8 30.6 %copy-start.15 = (bf16[2,16,1,4,128]{4,3,1,0,2:T(4,128)(2,1)}, bf16[2,16,1,4,128]{4,3,1,0,2:T(4,128)(2,1)S(1)}, u32[]{:S(2)}) copy-start(bf16[2,16,1,4,128]{4,3,1,0,2:T(4,128)(2,1)S(1)} %get-tuple-element.135) | copy-start | bytes 98308
  243.8 30.6 %copy-start.17 = (bf16[2,16,1,4,128]{4,3,1,0,2:T(4,128)(2,1)}, bf16[2,16,1,4,128]{4,3,1,0,2:T(4,128)(2,1)S(1)}, u32[]{:S(2)}) copy-start(bf16[2,16,1,4,128]{4,3,1,0,2:T(4,128)(2,1)S(1)} %get-tuple-element.136) | copy-start | bytes 98308
  244.6 24.1 %copy-start.38 = (f32[2,4,16]{2,1,0:T(4,128)}, f32[2,4,16]{2,1,0:T(4,128)S(1)}, u32[]{:S(2)}) copy-start(f32[2,4,16]{2,1,0:T(4,128)S(1)} %get-tuple-element.140) | copy-start | bytes 1540
  256.6 11.9 %collective-permute-start = (bf16[32,3072]{1,0:T(8,128)(2,1)S(1)}, bf16[32,3072]{1,0:T(8,128)(2,1)S(1)}, u32[]{:S(2)}, u32[]{:S(2)}) collective-permute-start(bf16[32,3072]{1,0:T(8,128)(2,1)S(1)} %fusion.133), channel_id=1, source_target_pairs={{0,16},{1,17},{2,18},{3,19},{4,20},{5,21},{6,22},{7,23},{8,24},{9,... | collective-permute-start | bytes 589832 | tf_op jit(solution)/shard_map/ppermute | solution.py:21
  275.3 19.8 %copy-start.40 = (f32[2,4,16]{2,1,0:T(4,128)}, f32[2,4,16]{2,1,0:T(4,128)S(1)}, u32[]{:S(2)}) copy-start(f32[2,4,16]{2,1,0:T(4,128)S(1)} %get-tuple-element.142) | copy-start | bytes 1540
  287.5 6.2 collective-permute-start.1
  295.1 9.7 %copy-start.29 = (f32[32]{0:T(128)}, f32[32]{0:T(128)S(1)}, u32[]{:S(2)}) copy-start(f32[32]{0:T(128)S(1)} %add_rsqrt_fusion.3) | copy-start | bytes 388
  300.7 22.4 %copy-start.23 = (bf16[2,16,1,4,128]{4,3,1,0,2:T(4,128)(2,1)}, bf16[2,16,1,4,128]{4,3,1,0,2:T(4,128)(2,1)S(1)}, u32[]{:S(2)}) copy-start(bf16[2,16,1,4,128]{4,3,1,0,2:T(4,128)(2,1)S(1)} %get-tuple-element.129) | copy-start | bytes 98308
  301.5 27.1 %copy-start.42 = (f32[2,4,16]{2,1,0:T(4,128)}, f32[2,4,16]{2,1,0:T(4,128)S(1)}, u32[]{:S(2)}) copy-start(f32[2,4,16]{2,1,0:T(4,128)S(1)} %get-tuple-element.144) | copy-start | bytes 1540
  301.8 21.2 %copy-start.3 = (bf16[2,16,4,128]{3,2,1,0:T(4,128)(2,1)}, bf16[2,16,4,128]{3,2,1,0:T(4,128)(2,1)S(1)}, u32[]{:S(2)}) copy-start(bf16[2,16,4,128]{3,2,1,0:T(4,128)(2,1)S(1)} %copy.131) | copy-start | bytes 98308
  313.6 9.0 %collective-permute-start.2 = (bf16[32,3072]{1,0:T(8,128)(2,1)S(1)}, bf16[32,3072]{1,0:T(8,128)(2,1)S(1)}, u32[]{:S(2)}, u32[]{:S(2)}) collective-permute-start(bf16[32,3072]{1,0:T(8,128)(2,1)S(1)} %fusion.128), channel_id=1, source_target_pairs={{0,16},{1,17},{2,18},{3,19},{4,20},{5,21},{6,22},{7,23},{8,24},{9,... | collective-permute-start | bytes 589832 | tf_op jit(solution)/shard_map/ppermute | solution.py:21
  328.6 19.9 %copy-start.4 = (bf16[2,16,4,128]{3,2,1,0:T(4,128)(2,1)S(1)}, bf16[2,16,4,128]{3,2,1,0:T(4,128)(2,1)}, u32[]{:S(2)}) copy-start(bf16[2,16,4,128]{3,2,1,0:T(4,128)(2,1)} %copy-done.3) | copy-start | bytes 98308
  328.7 22.2 %copy-start.27 = (bf16[2,16,1,4,128]{4,3,1,0,2:T(4,128)(2,1)}, bf16[2,16,1,4,128]{4,3,1,0,2:T(4,128)(2,1)S(1)}, u32[]{:S(2)}) copy-start(bf16[2,16,1,4,128]{4,3,1,0,2:T(4,128)(2,1)S(1)} %get-tuple-element.127) | copy-start | bytes 98308
  341.5 9.0 %collective-permute-start.3 = (bf16[32,3072]{1,0:T(8,128)(2,1)S(1)}, bf16[32,3072]{1,0:T(8,128)(2,1)S(1)}, u32[]{:S(2)}, u32[]{:S(2)}) collective-permute-start(bf16[32,3072]{1,0:T(8,128)(2,1)S(1)} %fusion.129), channel_id=1, source_target_pairs={{0,16},{1,17},{2,18},{3,19},{4,20},{5,21},{6,22},{7,23},{8,24},{9,... | collective-permute-start | bytes 589832 | tf_op jit(solution)/shard_map/ppermute | solution.py:21
  364.8 43.4 %copy-start.37 = (f32[2,4,16,16]{2,3,1,0:T(8,128)S(1)}, f32[2,4,16,16]{2,3,1,0:T(8,128)}, u32[]{:S(2)}) copy-start(f32[2,4,16,16]{2,3,1,0:T(8,128)} %get-tuple-element.147) | copy-start | bytes 24580
  364.8 43.4 %copy-start.45 = (f32[2,4,16]{2,1,0:T(4,128)S(1)}, f32[2,4,16]{2,1,0:T(4,128)}, u32[]{:S(2)}) copy-start(f32[2,4,16]{2,1,0:T(4,128)} %copy-done.44) | copy-start | bytes 1540
  364.8 43.6 %copy-start.28 = (bf16[2,16,1,4,128]{4,3,1,0,2:T(4,128)(2,1)S(1)}, bf16[2,16,1,4,128]{4,3,1,0,2:T(4,128)(2,1)}, u32[]{:S(2)}) copy-start(bf16[2,16,1,4,128]{4,3,1,0,2:T(4,128)(2,1)} %copy-done.27) | copy-start | bytes 98308
  364.8 82.6 %all-reduce.7.cloned.1.call-start = ((), (), s32[]{:S(2)}) async-start(), calls=%async_computation.3 | async-start | bytes 393216 | tf_op jit(solution)/shard_map/psum | solution.py:189
  397.9 7.6 collective-permute-start.4
  409.0 38.4 %copy-start.32 = (f32[32]{0:T(128)S(1)}, f32[32]{0:T(128)}, u32[]{:S(2)}) copy-start(f32[32]{0:T(128)} %copy-done.31) | copy-start | bytes 388
  409.0 50.9 %copy-start.14 = (bf16[2,16,1,4,128]{4,3,1,0,2:T(4,128)(2,1)S(1)}, bf16[2,16,1,4,128]{4,3,1,0,2:T(4,128)(2,1)}, u32[]{:S(2)}) copy-start(bf16[2,16,1,4,128]{4,3,1,0,2:T(4,128)(2,1)} %copy-done.13) | copy-start | bytes 98308
  409.0 51.0 %copy-start.24 = (bf16[2,16,1,4,128]{4,3,1,0,2:T(4,128)(2,1)S(1)}, bf16[2,16,1,4,128]{4,3,1,0,2:T(4,128)(2,1)}, u32[]{:S(2)}) copy-start(bf16[2,16,1,4,128]{4,3,1,0,2:T(4,128)(2,1)} %copy-done.23) | copy-start | bytes 98308
  409.0 51.0 %copy-start.36 = (f32[2,4,16,16]{2,3,1,0:T(8,128)S(1)}, f32[2,4,16,16]{2,3,1,0:T(8,128)}, u32[]{:S(2)}) copy-start(f32[2,4,16,16]{2,3,1,0:T(8,128)} %get-tuple-element.145) | copy-start | bytes 24580
  409.0 51.0 %copy-start.43 = (f32[2,4,16]{2,1,0:T(4,128)S(1)}, f32[2,4,16]{2,1,0:T(4,128)}, u32[]{:S(2)}) copy-start(f32[2,4,16]{2,1,0:T(4,128)} %copy-done.42) | copy-start | bytes 1540
  416.3 44.0 %copy-start.26 = (bf16[2,16,1,4,128]{4,3,1,0,2:T(4,128)(2,1)S(1)}, bf16[2,16,1,4,128]{4,3,1,0,2:T(4,128)(2,1)}, u32[]{:S(2)}) copy-start(bf16[2,16,1,4,128]{4,3,1,0,2:T(4,128)(2,1)} %copy-done.25) | copy-start | bytes 98308
  416.3 82.9 %all-reduce.9.cloned.1.call-start = ((), (), s32[]{:S(2)}) async-start(), calls=%async_computation.4 | async-start | bytes 393216 | tf_op jit(solution)/shard_map/psum | solution.py:189
  449.8 7.6 collective-permute-start.5
  460.9 38.3 %copy-start.30 = (f32[32]{0:T(128)S(1)}, f32[32]{0:T(128)}, u32[]{:S(2)}) copy-start(f32[32]{0:T(128)} %copy-done.29) | copy-start | bytes 388
  468.1 43.6 %copy-start.12 = (bf16[2,16,1,4,128]{4,3,1,0,2:T(4,128)(2,1)S(1)}, bf16[2,16,1,4,128]{4,3,1,0,2:T(4,128)(2,1)}, u32[]{:S(2)}) copy-start(bf16[2,16,1,4,128]{4,3,1,0,2:T(4,128)(2,1)} %copy-done.11) | copy-start | bytes 98308
  468.1 43.8 %copy-start.20 = (bf16[2,16,1,4,128]{4,3,1,0,2:T(4,128)(2,1)S(1)}, bf16[2,16,1,4,128]{4,3,1,0,2:T(4,128)(2,1)}, u32[]{:S(2)}) copy-start(bf16[2,16,1,4,128]{4,3,1,0,2:T(4,128)(2,1)} %copy-done.19) | copy-start | bytes 98308
  468.1 43.8 %copy-start.35 = (f32[2,4,16,16]{2,3,1,0:T(8,128)S(1)}, f32[2,4,16,16]{2,3,1,0:T(8,128)}, u32[]{:S(2)}) copy-start(f32[2,4,16,16]{2,3,1,0:T(8,128)} %get-tuple-element.143) | copy-start | bytes 24580
  468.1 43.8 %copy-start.41 = (f32[2,4,16]{2,1,0:T(4,128)S(1)}, f32[2,4,16]{2,1,0:T(4,128)}, u32[]{:S(2)}) copy-start(f32[2,4,16]{2,1,0:T(4,128)} %copy-done.40) | copy-start | bytes 1540
  468.1 44.0 %copy-start.22 = (bf16[2,16,1,4,128]{4,3,1,0,2:T(4,128)(2,1)S(1)}, bf16[2,16,1,4,128]{4,3,1,0,2:T(4,128)(2,1)}, u32[]{:S(2)}) copy-start(bf16[2,16,1,4,128]{4,3,1,0,2:T(4,128)(2,1)} %copy-done.21) | copy-start | bytes 98308
  468.2 83.0 %all-reduce.11.cloned.1.call-start = ((), (), s32[]{:S(2)}) async-start(), calls=%async_computation.5 | async-start | bytes 393216 | tf_op jit(solution)/shard_map/psum | solution.py:189
  501.6 7.6 collective-permute-start.6
  512.8 7.4 copy-start.2
  520.1 44.3 %copy-start.10 = (bf16[2,16,1,4,128]{4,3,1,0,2:T(4,128)(2,1)S(1)}, bf16[2,16,1,4,128]{4,3,1,0,2:T(4,128)(2,1)}, u32[]{:S(2)}) copy-start(bf16[2,16,1,4,128]{4,3,1,0,2:T(4,128)(2,1)} %copy-done.9) | copy-start | bytes 98308
  520.1 44.4 %copy-start.16 = (bf16[2,16,1,4,128]{4,3,1,0,2:T(4,128)(2,1)S(1)}, bf16[2,16,1,4,128]{4,3,1,0,2:T(4,128)(2,1)}, u32[]{:S(2)}) copy-start(bf16[2,16,1,4,128]{4,3,1,0,2:T(4,128)(2,1)} %copy-done.15) | copy-start | bytes 98308
  520.1 44.4 %copy-start.34 = (f32[2,4,16,16]{2,3,1,0:T(8,128)S(1)}, f32[2,4,16,16]{2,3,1,0:T(8,128)}, u32[]{:S(2)}) copy-start(f32[2,4,16,16]{2,3,1,0:T(8,128)} %get-tuple-element.141) | copy-start | bytes 24580
  520.1 44.4 %copy-start.39 = (f32[2,4,16]{2,1,0:T(4,128)S(1)}, f32[2,4,16]{2,1,0:T(4,128)}, u32[]{:S(2)}) copy-start(f32[2,4,16]{2,1,0:T(4,128)} %copy-done.38) | copy-start | bytes 1540
  520.1 44.6 %copy-start.18 = (bf16[2,16,1,4,128]{4,3,1,0,2:T(4,128)(2,1)S(1)}, bf16[2,16,1,4,128]{4,3,1,0,2:T(4,128)(2,1)}, u32[]{:S(2)}) copy-start(bf16[2,16,1,4,128]{4,3,1,0,2:T(4,128)(2,1)} %copy-done.17) | copy-start | bytes 98308
  520.1 273.6 %reduce-scatter.2.cloned.1.call-start = ((), (), s32[]{:S(2)}) async-start(), calls=%async_computation.6 | async-start | bytes 15728640 | tf_op jit(solution)/shard_map/reduce_scatter | solution.py:222
  553.5 7.6 collective-permute-start.7
  (12 other events, 32.9 us)
Sparse Core Ops, SparseCore 0:
  12.3 220.9 all-gather.5
  365.0 30.5 all-reduce.4
  416.4 30.9 all-reduce.6
  468.3 30.9 all-reduce.8
  520.2 30.9 all-reduce.10
  582.5 211.1 reduce-scatter.1
